TPU v7x, 512 devices: a whole 4x4x16 slice. The times are simulated.
512 devices in a mesh: dp: 4 (over x_hi, core), expert: 128 (over y, z, x_lo).
Axes of the slice: x: 4 (x_hi: 2, x_lo: 2; x = x_hi * 2 + x_lo), y: 4, z: 16, core: 2. Of those that a mesh axis runs over, the one named last changes fastest.
Arguments:
- gradient: bfloat16 [4, 64, 2048, 768], P('dp', None, 'expert'), may hold values from -6 to 6
- momentum: float32 [64, 2048, 768], P('dp', 'expert'), may hold values from -31 to 31
Outputs:
- new_momentum: float32 [64, 2048, 768], P('dp', 'expert')
- update: float32 [64, 2048, 768], P('dp', 'expert')
All inputs are finite; a program needn't handle non-finite values.
Results may differ from a plain program's by a relative error of at most 0.0003.
Values sent between devices are 32-bit elements; how exact they have to be, the bound alone decides.
A program may use at most 64 MiB of HBM per device.

v0:
```python
import jax
import jax.numpy as jnp
from jax import lax
from jax.sharding import PartitionSpec as P

D = 2048
ITERS = 2


first_coeff = 3.4445
second_coeff = -4.775
third_coeff = 2.0315
momentum_keep = 0.95
norm_epsilon = 1e-07


def partner(value, axis, apart):
    mask = 2**apart
    pairs = [(source, source ^ mask) for source in range(lax.axis_size(axis))]
    return lax.ppermute(value, axis, pairs)


def total_gram(local_gram, group_bits):
    running = local_gram
    for level_bit in group_bits:
        running = running + partner(running, "expert", level_bit)
    return running


def highest_dot(left, right):
    return jnp.dot(left, right, precision=lax.Precision.HIGHEST, preferred_element_type=jnp.float32)


def shards(gradient, momentum):
    exp_local, row_shard, columns = momentum.shape
    axis_width = lax.axis_size("expert")
    owners = axis_width // exp_local
    per_owner = row_shard // owners
    summed = lax.psum_scatter(gradient.astype(jnp.float32), "dp", scatter_dimension=1, tiled=True)
    new_momentum = momentum_keep * momentum + summed[0]
    pieces = new_momentum.reshape(exp_local, owners, per_owner, columns)
    position = lax.axis_index("expert")
    owner_bits = owners.bit_length() - 1
    outgoing = pieces.transpose(1, 0, 2, 3).reshape(axis_width, per_owner, columns)
    lowest_bit = exp_local.bit_length() - 1
    group_bits = [lowest_bit + offset_bit for offset_bit in range(owner_bits)]
    own_expert = position % exp_local
    square_sum = None
    shard_sums = jnp.sum(new_momentum * new_momentum, axis=(1, 2))
    totals = lax.psum(shard_sums, "expert")
    picked = jnp.where(jnp.arange(exp_local, dtype=jnp.int32) == own_expert, totals, 0.0)
    square_sum = jnp.sum(picked)
    arrived = lax.all_to_all(outgoing, "expert", split_axis=0, concat_axis=0, tiled=True)
    iterate = arrived.reshape(axis_width * per_owner, columns)
    for repeat_index in range(ITERS):
        summed_gram = total_gram(highest_dot(iterate.T, iterate), group_bits)
        if repeat_index == 0:
            factor = 1.0 / (jnp.sqrt(square_sum) + norm_epsilon)
        else:
            factor = 1.0
        scaled = summed_gram * (factor * factor)
        polynomial = second_coeff * scaled + third_coeff * highest_dot(scaled, scaled)
        iterate = factor * (first_coeff * iterate + highest_dot(iterate, polynomial))
    update = D**0.5 * iterate
    returned = lax.all_to_all(
        update.reshape(axis_width, per_owner, columns),
        "expert",
        split_axis=0,
        concat_axis=0,
        tiled=True,
    )
    local_update = (
        returned.reshape(owners, exp_local, per_owner, columns)
        .transpose(1, 0, 2, 3)
        .reshape(exp_local, row_shard, columns)
    )
    return (new_momentum, local_update)


def solution(mesh):
    placed = (P("dp", None, "expert", None), P("dp", "expert", None))
    return jax.shard_map(
        shards,
        mesh=mesh,
        in_specs=placed,
        out_specs=(P("dp", "expert", None), P("dp", "expert", None)),
        check_vma=False,
    )
```

profile of v0, /device:TPU:2, one launch (start us, length us, event | category | flops | bytes accessed | tf_op | source)
XLA Modules:
  0.0 1045.1 jit_solution(10491692984689795582)
XLA Ops:
  7.2 0.0 reduce-scatter.2.cloned.1.call-start
  7.2 3.5 convert_element_type.3
  10.7 0.0 copy-start.2
  10.7 0.0 reduce-scatter.2.cloned.1.call-update
  10.7 64.2 %reduce-scatter.2.cloned.1.call-done = f32[1,16,16,768]{3,2,1,0:T(8,128)} async-done(((f32[1,64,16,768]{3,2,1,0:T(8,128)}), f32[1,16,16,768]{3,2,1,0:T(8,128)}) %reduce-scatter.2.cloned.1.call-update) | async-done | bytes 786448 | tf_op jit(solution)/shard_map/reduce_scatter | solution.py:39
  74.9 0.0 copy-done.2
  74.9 1.4 multiply_reduce_fusion
  76.3 0.0 copy-start
  76.3 0.5 reshape.22
  76.8 0.1 copy.11
  76.9 61.3 %all_to_all.10 = f32[128,2,768]{2,1,0:T(2,128)S(1)} all-to-all(f32[128,2,768]{2,1,0:T(2,128)S(1)} %bitcast.16), channel_id=1, replica_groups=mesh['dp'=4,'expert'=128] {'expert'}, dimensions={0} | all-to-all | bytes 1572864 | tf_op jit(solution)/shard_map/all_to_all | solution.py:53
  138.2 0.0 copy-done
  138.2 2.2 convolution_bitcast_fusion
  140.4 4.1 collective-permute-start
  144.5 180.6 %collective-permute-done = f32[768,768]{1,0:T(8,128)S(1)} collective-permute-done((f32[768,768]{1,0:T(8,128)S(1)}, f32[768,768]{1,0:T(8,128)S(1)}, u32[]{:S(2)}, u32[]{:S(2)}) %collective-permute-start) | collective-permute-done | bytes 2359328 | tf_op jit(solution)/shard_map/ppermute | solution.py:20
  325.1 0.3 add.47
  325.4 32.9 %collective-permute-start.1 = (f32[768,768]{1,0:T(8,128)S(1)}, f32[768,768]{1,0:T(8,128)S(1)}, u32[]{:S(2)}, u32[]{:S(2)}) collective-permute-start(f32[768,768]{1,0:T(8,128)S(1)} %add.47), channel_id=1, source_target_pairs={{0,32},{1,33},{2,34},{3,35},{4,36},{5,37},{6,38},{7,39},{8,40},{9,... | collective-permute-start | bytes 7077896 | tf_op jit(solution)/shard_map/ppermute | solution.py:20
  358.3 48.7 %collective-permute-done.1 = f32[768,768]{1,0:T(8,128)S(1)} collective-permute-done((f32[768,768]{1,0:T(8,128)S(1)}, f32[768,768]{1,0:T(8,128)S(1)}, u32[]{:S(2)}, u32[]{:S(2)}) %collective-permute-start.1) | collective-permute-done | bytes 2359328 | tf_op jit(solution)/shard_map/ppermute | solution.py:20
  407.0 0.3 add.48
  407.3 4.6 collective-permute-start.2
  411.9 378.2 %psum.7 = f32[16]{0:T(128)S(1)} all-reduce(f32[16]{0:T(128)S(1)} %get-tuple-element.2), channel_id=1, replica_groups=mesh['dp'=4,'expert'=128] {'expert'}, use_global_device_ids=true, to_apply=%region_2.3 | all-reduce | flops 16 | bytes 128 | tf_op jit(solution)/shard_map/psum | solution.py:50
  790.1 0.6 fusion.23
  791.4 1.4 reshape.24
  792.8 0.0 copy-start.1
  792.8 0.0 collective-permute-done.2
  792.8 8.6 fusion.21
  801.4 0.0 copy-done.1
  801.4 4.3 fusion.11
  805.7 2.2 fusion.30
  808.0 1.9 collective-permute-start.3
  809.9 74.3 %collective-permute-done.3 = f32[768,768]{1,0:T(8,128)S(1)} collective-permute-done((f32[768,768]{1,0:T(8,128)S(1)}, f32[768,768]{1,0:T(8,128)S(1)}, u32[]{:S(2)}, u32[]{:S(2)}) %collective-permute-start.3) | collective-permute-done | bytes 2359328 | tf_op jit(solution)/shard_map/ppermute | solution.py:20
  884.2 0.3 add.52
  884.5 1.9 collective-permute-start.4
  886.4 29.1 %collective-permute-done.4 = f32[768,768]{1,0:T(8,128)S(1)} collective-permute-done((f32[768,768]{1,0:T(8,128)S(1)}, f32[768,768]{1,0:T(8,128)S(1)}, u32[]{:S(2)}, u32[]{:S(2)}) %collective-permute-start.4) | collective-permute-done | bytes 2359328 | tf_op jit(solution)/shard_map/ppermute | solution.py:20
  915.5 0.3 add.53
  915.8 2.1 collective-permute-start.5
  918.0 30.1 %collective-permute-done.5 = f32[768,768]{1,0:T(8,128)S(1)} collective-permute-done((f32[768,768]{1,0:T(8,128)S(1)}, f32[768,768]{1,0:T(8,128)S(1)}, u32[]{:S(2)}, u32[]{:S(2)}) %collective-permute-start.5) | collective-permute-done | bytes 2359328 | tf_op jit(solution)/shard_map/ppermute | solution.py:20
  948.0 6.0 fusion.18
  954.0 2.5 add_multiply_fusion.3
  956.6 0.5 reshape.25
  957.0 79.7 %all_to_all.11 = f32[128,2,768]{2,1,0:T(2,128)S(1)} all-to-all(f32[128,2,768]{2,1,0:T(2,128)S(1)} %reshape.25), channel_id=1, replica_groups=mesh['dp'=4,'expert'=128] {'expert'}, dimensions={0} | all-to-all | bytes 1572864 | tf_op jit(solution)/shard_map/all_to_all | solution.py:65
  1036.7 0.1 copy.18
  1036.8 1.4 reshape.27
Async XLA Ops:
  7.2 67.8 %reduce-scatter.2.cloned.1.call-start = ((), (), s32[]{:S(2)}) async-start(), calls=%async_computation.3 | async-start | bytes 3932160 | tf_op jit(solution)/shard_map/reduce_scatter | solution.py:39
  10.7 64.2 %copy-start.2 = (f32[16,16,768]{2,1,0:T(8,128)S(1)}, f32[16,16,768]{2,1,0:T(8,128)}, u32[]{:S(2)}) copy-start(f32[16,16,768]{2,1,0:T(8,128)} %param.3) | copy-start | bytes 2359300
  76.3 61.9 %copy-start = (f32[16,16,768]{2,1,0:T(8,128)}, f32[16,16,768]{2,1,0:T(8,128)S(1)}, u32[]{:S(2)}) copy-start(f32[16,16,768]{2,1,0:T(8,128)S(1)} %get-tuple-element.3) | copy-start | bytes 2359300
  140.4 184.7 %collective-permute-start = (f32[768,768]{1,0:T(8,128)S(1)}, f32[768,768]{1,0:T(8,128)S(1)}, u32[]{:S(2)}, u32[]{:S(2)}) collective-permute-start(f32[768,768]{1,0:T(8,128)S(1)} %convolution_bitcast_fusion), channel_id=1, source_target_pairs={{0,16},{1,17},{2,18},{3,19},{4,20},{5,21},{6,22},{7,23},{8,24},{9,... | collective-permute-start | bytes 7077896 | tf_op jit(solution)/shard_map/ppermute | solution.py:20
  325.4 81.6 %collective-permute-start.1 = (f32[768,768]{1,0:T(8,128)S(1)}, f32[768,768]{1,0:T(8,128)S(1)}, u32[]{:S(2)}, u32[]{:S(2)}) collective-permute-start(f32[768,768]{1,0:T(8,128)S(1)} %add.47), channel_id=1, source_target_pairs={{0,32},{1,33},{2,34},{3,35},{4,36},{5,37},{6,38},{7,39},{8,40},{9,... | collective-permute-start | bytes 7077896 | tf_op jit(solution)/shard_map/ppermute | solution.py:20
  407.3 385.5 %collective-permute-start.2 = (f32[768,768]{1,0:T(8,128)S(1)}, f32[768,768]{1,0:T(8,128)}, u32[]{:S(2)}, u32[]{:S(2)}) collective-permute-start(f32[768,768]{1,0:T(8,128)S(1)} %add.48), channel_id=1, source_target_pairs={{0,64},{1,65},{2,66},{3,67},{4,68},{5,69},{6,70},{7,71},{8,72},{9,... | collective-permute-start | bytes 7077896 | tf_op jit(solution)/shard_map/ppermute | solution.py:20
  792.8 8.6 copy-start.1
  808.0 76.2 %collective-permute-start.3 = (f32[768,768]{1,0:T(8,128)S(1)}, f32[768,768]{1,0:T(8,128)S(1)}, u32[]{:S(2)}, u32[]{:S(2)}) collective-permute-start(f32[768,768]{1,0:T(8,128)S(1)} %fusion.30), channel_id=1, source_target_pairs={{0,16},{1,17},{2,18},{3,19},{4,20},{5,21},{6,22},{7,23},{8,24},{9,... | collective-permute-start | bytes 7077896 | tf_op jit(solution)/shard_map/ppermute | solution.py:20
  884.5 31.0 %collective-permute-start.4 = (f32[768,768]{1,0:T(8,128)S(1)}, f32[768,768]{1,0:T(8,128)S(1)}, u32[]{:S(2)}, u32[]{:S(2)}) collective-permute-start(f32[768,768]{1,0:T(8,128)S(1)} %add.52), channel_id=1, source_target_pairs={{0,32},{1,33},{2,34},{3,35},{4,36},{5,37},{6,38},{7,39},{8,40},{9,... | collective-permute-start | bytes 7077896 | tf_op jit(solution)/shard_map/ppermute | solution.py:20
  915.8 32.2 %collective-permute-start.5 = (f32[768,768]{1,0:T(8,128)S(1)}, f32[768,768]{1,0:T(8,128)S(1)}, u32[]{:S(2)}, u32[]{:S(2)}) collective-permute-start(f32[768,768]{1,0:T(8,128)S(1)} %add.53), channel_id=1, source_target_pairs={{0,64},{1,65},{2,66},{3,67},{4,68},{5,69},{6,70},{7,71},{8,72},{9,... | collective-permute-start | bytes 7077896 | tf_op jit(solution)/shard_map/ppermute | solution.py:20
Sparse Core Ops, SparseCore 0:
  11.1 63.8 reduce-scatter.1
where the time goes:
time: 1050 us
  blocking collectives  519 us (49%)
  waiting for transfers between devices  427 us (41%)
  starting transfers between devices  47.5 us (5%)
  matrix products  25.8 us (2%)
  between operations  14.9 us (1%)
    psum x1, blocking collectives, shards(): totals = lax.psum(shard_sums, 'expert')  378 us
    ppermute x6, waiting for transfers between devices, partner(): return lax.ppermute(value, axis, pairs)  363 us
    all_to_all x1, blocking collectives, shards(): lax.all_to_all(update.reshape(axis_width, per_owner, columns), 'expert',...  79.7 us
    reduce_scatter x1, waiting for transfers between devices, shards(): lax.psum_scatter(gradient.astype(jnp.float32), 'dp', scatter_dimension=1,...  64.2 us
    all_to_all x1, blocking collectives, shards(): lax.all_to_all(outgoing, 'expert', split_axis=0, concat_axis=0, tiled=True)  61.3 us
    ppermute x6, starting transfers between devices, partner(): return lax.ppermute(value, axis, pairs)  47.5 us
    dot_general x6, matrix products, highest_dot(): jnp.dot(left, right, precision=lax.Precision.HIGHEST, preferred_element_t...  25.8 us
  transfers between devices with their start and end apart: 7, of which 6 were waited for; matrix products, arithmetic and copies ran while one was open for 0% of the time, Pallas kernels for 0%

commit v1 on v0

v1 whole, which is shorter than its diff:
```python
import jax
import jax.numpy as jnp
from jax import lax
from jax.experimental import pallas as pl
from jax.experimental.pallas import tpu as pltpu
from jax.sharding import PartitionSpec as P

D = 2048
FF = 768

first_coeff = 3.4445
second_coeff = -4.775
third_coeff = 2.0315
momentum_keep = 0.95
norm_epsilon = 1e-07

NY, NZ = 4, 16
EXP = 16
ROWS = 16
WAVES = 4
PER = EXP // WAVES
BLK = 256
PAIRS = ((0, 0), (0, 1), (0, 2), (1, 1), (1, 2), (2, 2))
DIAGONAL = (0, 3, 5)
HALF = 3 * BLK
PIECE = HALF // NY

MESH = pl.DeviceIdType.MESH
f32 = jnp.float32
bf16 = jnp.bfloat16


def split(value):
    high = value.astype(bf16)
    return high, (value - high.astype(f32)).astype(bf16)


def dot(left, right):
    return jnp.dot(left, right, preferred_element_type=f32)


def dot_rows(left, right):
    return lax.dot_general(left, right, (((0,), (0,)), ((), ())), preferred_element_type=f32)


def kernel(
    grad,
    mom,
    new_mom,
    upd,
    core_out,
    core_in,
    x_out,
    x_in,
    rows,
    gram,
    gram_core,
    half,
    gram_y,
    full,
    s_hi,
    s_lo,
    q_hi,
    q_lo,
    result,
    core_ss,
    core_rs,
    x_ss,
    x_rs,
    fwd_ss,
    fwd_rs,
    ret_ss,
    ret_rs,
    gc_ss,
    gc_rs,
    gy_ss,
    gy_rs,
    ay_ss,
    ay_rs,
    ac_ss,
    ac_rs,
):
    dp = lax.axis_index("dp")
    ex = lax.axis_index("expert")
    h, c = dp // 2, dp % 2
    y, z, a = ex // 32, (ex // 2) % NZ, ex % 2

    other_core = (h * 2 + 1 - c, ex)
    x_partner = ((1 - h) * 2 + c, ex)

    def z_peer(i):
        return (h * 2 + a, y * 32 + i * 2 + c)

    def y_peer(k):
        return (dp, ((y + k) % NY) * 32 + z * 2 + a)

    def remote(src, dst, ss, rs, to):
        return pltpu.make_async_remote_copy(
            src_ref=src, dst_ref=dst, send_sem=ss, recv_sem=rs, device_id=to, device_id_type=MESH
        )

    straight = a == c

    barrier = pltpu.get_barrier_semaphore()

    def greet(to):
        pl.semaphore_signal(barrier, inc=1, device_id=to, device_id_type=MESH)

    greet(other_core)
    greet(x_partner)
    for k in range(1, NY):
        greet(y_peer(k))
    for i in range(NZ):

        @pl.when(jnp.logical_not(jnp.logical_and(straight, z == i)))
        def _():
            greet(z_peer(i))

    pl.semaphore_wait(barrier, 5 + NZ - straight.astype(jnp.int32))

    def core_copy(side, w):
        return remote(core_out.at[side, w], core_in.at[side, w], core_ss.at[side, w], core_rs.at[side, w], other_core)

    def x_copy(w):
        return remote(x_out.at[w], x_in.at[w], x_ss.at[w], x_rs.at[w], x_partner)

    def base(side, core):
        owner_h = 1 - h if side == 0 else h
        return (owner_h * 2 + core) * EXP

    for w in range(WAVES):
        for side in range(2):
            for j in range(PER):
                core_out[side, w, j] = grad[0, base(side, 1 - c) + WAVES * j + w].astype(f32)
            core_copy(side, w).start()
    for w in range(WAVES):
        core_copy(0, w).wait_recv()
        for j in range(PER):
            x_out[w, j] = grad[0, base(0, c) + WAVES * j + w].astype(f32) + core_in[0, w, j]
        x_copy(w).start()
    for w in range(WAVES):
        core_copy(1, w).wait_recv()
        for j in range(PER):
            i = WAVES * j + w
            new_mom[i] = momentum_keep * mom[i] + (grad[0, base(1, c) + i].astype(f32) + core_in[1, w, j])

    def fwd_copy(i, slot):
        return remote(new_mom.at[i], rows.at[slot], fwd_ss.at[i], fwd_rs.at[slot], z_peer(i))

    for w in range(WAVES):
        x_copy(w).wait_recv()
        for j in range(PER):
            i = WAVES * j + w
            new_mom[i] = new_mom[i] + x_in[w, j]
            here = jnp.logical_and(straight, z == i)

            @pl.when(here)
            def _():
                rows[i] = new_mom[i]

            @pl.when(jnp.logical_not(here))
            def _():
                fwd_copy(i, z).start()

    for s in range(NZ):

        @pl.when(jnp.logical_not(jnp.logical_and(straight, z == s)))
        def _():
            fwd_copy(s, s).wait_recv()

    x0 = rows[...].reshape(NZ * ROWS, FF)
    x_hi, x_lo = split(x0)
    for b, (p, q) in enumerate(PAIRS):
        ph, plo = x_hi[:, p * BLK : (p + 1) * BLK], x_lo[:, p * BLK : (p + 1) * BLK]
        qh, qlo = x_hi[:, q * BLK : (q + 1) * BLK], x_lo[:, q * BLK : (q + 1) * BLK]
        gram[b] = dot_rows(ph, qh) + (dot_rows(ph, qlo) + dot_rows(plo, qh))

    gc = remote(gram.at[pl.ds(3 * (1 - c), 3)], gram_core, gc_ss, gc_rs, other_core)
    gc.start()
    gc.wait_recv()
    for k in range(3):
        half[pl.ds(k * BLK, BLK)] = gram[3 * c + k] + gram_core[k]

    def piece(p):
        return pl.ds(pl.multiple_of(p * PIECE, PIECE), PIECE)

    def gy_copy(k):
        return remote(half.at[piece((y + k) % NY)], gram_y.at[k - 1], gy_ss.at[k - 1], gy_rs.at[k - 1], y_peer(k))

    for k in range(1, NY):
        gy_copy(k).start()
    for k in range(1, NY):
        gy_copy(k).wait_recv()
    own = piece(y)
    full[c, own] = (half[own] + gram_y[0]) + (gram_y[1] + gram_y[2])

    def ay_copy(k, p):
        return remote(full.at[c, piece(p)], full.at[c, piece(p)], ay_ss.at[k - 1], ay_rs.at[k - 1], y_peer(k))

    def ac_copy(k, core):
        p = piece((y + NY - k) % NY)
        return remote(full.at[core, p], full.at[core, p], ac_ss.at[k], ac_rs.at[k], other_core)

    for k in range(1, NY):
        ay_copy(k, y).start()
    ac_copy(0, c).start()
    for k in range(1, NY):
        ay_copy(k, (y + NY - k) % NY).wait_recv()
        ac_copy(k, c).start()
    for k in range(NY):
        ac_copy(k, 1 - c).wait_recv()

    def block(b):
        return full[b // 3, (b % 3) * BLK : (b % 3 + 1) * BLK, :]

    eye = lax.broadcasted_iota(jnp.int32, (BLK, BLK), 0) == lax.broadcasted_iota(jnp.int32, (BLK, BLK), 1)
    on_diagonal = jnp.where(eye, block(0) + block(3) + block(5), 0.0)
    square_sum = jnp.sum(jnp.sum(on_diagonal, axis=1, keepdims=True), axis=0, keepdims=True)
    factor = 1.0 / (jnp.sqrt(square_sum) + norm_epsilon)
    scale = factor * factor

    def put(hi, lo, p, q, value):
        vh, vl = split(value)
        hi[p * BLK : (p + 1) * BLK, q * BLK : (q + 1) * BLK] = vh
        lo[p * BLK : (p + 1) * BLK, q * BLK : (q + 1) * BLK] = vl

    for b, (p, q) in enumerate(PAIRS):
        value = block(b) * scale
        put(s_hi, s_lo, p, q, value)
        if p != q:
            put(s_hi, s_lo, q, p, value.T)
    for b, (p, q) in enumerate(PAIRS):
        lh, ll = s_hi[p * BLK : (p + 1) * BLK, :], s_lo[p * BLK : (p + 1) * BLK, :]
        rh, rl = s_hi[:, q * BLK : (q + 1) * BLK], s_lo[:, q * BLK : (q + 1) * BLK]
        square = dot(lh, rh) + (dot(lh, rl) + dot(ll, rh))
        value = (second_coeff * scale) * block(b) + third_coeff * square
        if p == q:
            value = value + jnp.where(eye, first_coeff, 0.0)
        put(q_hi, q_lo, p, q, value)
        if p != q:
            put(q_hi, q_lo, q, p, value.T)

    def times(value, hi, lo):
        vh, vl = split(value)
        return dot(vh, hi[...]) + (dot(vh, lo[...]) + dot(vl, hi[...]))

    x1 = times(x0, q_hi, q_lo) * factor
    t1 = times(times(times(x1, q_hi, q_lo), s_hi, s_lo), q_hi, q_lo)
    t2 = times(times(times(t1, q_hi, q_lo), s_hi, s_lo), q_hi, q_lo)
    final = D**0.5 * (first_coeff * x1 + second_coeff * t1 + third_coeff * t2)
    result[...] = final.reshape(NZ, ROWS, FF)

    def ret_copy(s, slot):
        return remote(result.at[s], upd.at[slot], ret_ss.at[s], ret_rs.at[slot], z_peer(s))

    for s in range(NZ):
        here = jnp.logical_and(straight, z == s)

        @pl.when(here)
        def _():
            upd[s] = result[s]

        @pl.when(jnp.logical_not(here))
        def _():
            ret_copy(s, z).start()

    for w in range(WAVES):
        for side in range(2):
            core_copy(side, w).wait_send()
        x_copy(w).wait_send()
    gc.wait_send()
    for k in range(1, NY):
        gy_copy(k).wait_send()
        ay_copy(k, y).wait_send()
    for k in range(NY):
        ac_copy(k, c).wait_send()
    for s in range(NZ):

        @pl.when(jnp.logical_not(jnp.logical_and(straight, z == s)))
        def _():
            fwd_copy(s, s).wait_send()
            ret_copy(s, s).wait_send()
            ret_copy(s, s).wait_recv()


def shards(gradient, momentum):
    vmem = pl.BlockSpec(memory_space=pltpu.VMEM)
    dma = pltpu.SemaphoreType.DMA
    shape = jax.ShapeDtypeStruct(momentum.shape, f32)
    return pl.pallas_call(
        kernel,
        out_shape=(shape, shape),
        in_specs=[vmem, vmem],
        out_specs=(vmem, vmem),
        scratch_shapes=[
            pltpu.VMEM((2, WAVES, PER, ROWS, FF), f32),
            pltpu.VMEM((2, WAVES, PER, ROWS, FF), f32),
            pltpu.VMEM((WAVES, PER, ROWS, FF), f32),
            pltpu.VMEM((WAVES, PER, ROWS, FF), f32),
            pltpu.VMEM((NZ, ROWS, FF), f32),
            pltpu.VMEM((6, BLK, BLK), f32),
            pltpu.VMEM((3, BLK, BLK), f32),
            pltpu.VMEM((HALF, BLK), f32),
            pltpu.VMEM((NY - 1, PIECE, BLK), f32),
            pltpu.VMEM((2, HALF, BLK), f32),
            pltpu.VMEM((FF, FF), bf16),
            pltpu.VMEM((FF, FF), bf16),
            pltpu.VMEM((FF, FF), bf16),
            pltpu.VMEM((FF, FF), bf16),
            pltpu.VMEM((NZ, ROWS, FF), f32),
            dma((2, WAVES)),
            dma((2, WAVES)),
            dma((WAVES,)),
            dma((WAVES,)),
            dma((NZ,)),
            dma((NZ,)),
            dma((NZ,)),
            dma((NZ,)),
            dma,
            dma,
            dma((NY - 1,)),
            dma((NY - 1,)),
            dma((NY - 1,)),
            dma((NY - 1,)),
            dma((NY,)),
            dma((NY,)),
        ],
        compiler_params=pltpu.CompilerParams(
            collective_id=0, has_side_effects=True, vmem_limit_bytes=48 * 2**20
        ),
        name="muon",
    )(gradient, momentum)


def solution(mesh):
    placed = (P("dp", None, "expert", None), P("dp", "expert", None))
    return jax.shard_map(
        shards,
        mesh=mesh,
        in_specs=placed,
        out_specs=(P("dp", "expert", None), P("dp", "expert", None)),
        check_vma=False,
    )
```

time: 1050 us -> 140 us (0.13)
  the two profiles are of different devices: /device:TPU:2 before, /device:TPU:448 now
where the time goes in v1:
time: 140 us
  Pallas kernels  135 us (96%)
  local copies, waits for them, and re-layouts  4.29 us (3%)
    pallas_call x1, Pallas kernels, shards(): pl.pallas_call(kernel, out_shape=(shape, shape), in_specs=[vmem, vmem], o...  135 us
    unnamed x6, local copies, waits for them, and re-layouts  4.29 us

profile of v1, /device:TPU:448, one launch (start us, length us, event | category | flops | bytes accessed | tf_op | source)
XLA Modules:
  0.0 139.9 jit_solution(7860751689473331192)
XLA Ops:
  0.6 0.0 copy-start
  0.6 1.4 copy-done
  2.0 0.0 copy-start.1
  2.0 1.1 copy-done.1
  3.2 135.0 %muon.1 = (f32[16,16,768]{2,1,0:T(8,128)S(1)}, f32[16,16,768]{2,1,0:T(8,128)S(1)}) custom-call(bf16[1,64,16,768]{3,2,1,0:T(8,128)(2,1)S(1)} %copy-done, f32[16,16,768]{2,1,0:T(8,128)S(1)} %copy-done.1), custom_call_target="tpu_custom_call" | custom-call | tf_op jit(solution)/shard_map/muon/pallas_call | solution.py:290
  138.2 0.9 copy.6
  139.0 0.9 copy.7
Async XLA Ops:
  0.6 1.4 %copy-start = (bf16[1,64,16,768]{3,2,1,0:T(8,128)(2,1)S(1)}, bf16[1,64,16,768]{3,2,1,0:T(8,128)(2,1)}, u32[]{:S(2)}) copy-start(bf16[1,64,16,768]{3,2,1,0:T(8,128)(2,1)} %grad.1) | copy-start | bytes 4718596
  2.0 1.1 copy-start.1

commit v2 on v1

v2 whole, which is shorter than its diff:
```python
import functools

import jax
import jax.numpy as jnp
from jax import lax
from jax.experimental import pallas as pl
from jax.experimental.pallas import tpu as pltpu
from jax.sharding import PartitionSpec as P

D = 2048
FF = 768

first_coeff = 3.4445
second_coeff = -4.775
third_coeff = 2.0315
momentum_keep = 0.95
norm_epsilon = 1e-07

NY, NZ = 4, 16
EXP = 16
ROWS = 16
WAVES = 4
PER = EXP // WAVES
BLK = 256
PAIRS = ((0, 0), (0, 1), (0, 2), (1, 1), (1, 2), (2, 2))
DIAGONAL = (0, 3, 5)
HALF = 3 * BLK
PIECE = HALF // NY
HALF_PIECE = PIECE // 2

XAHEAD = 2
MESH = pl.DeviceIdType.MESH
f32 = jnp.float32
bf16 = jnp.bfloat16


def split(value):
    high = value.astype(bf16)
    return high, (value - high.astype(f32)).astype(bf16)


def dot(left, right):
    return jnp.dot(left, right, preferred_element_type=f32)


def dot_rows(left, right):
    return lax.dot_general(left, right, (((0,), (0,)), ((), ())), preferred_element_type=f32)


def kernel(
    grad_hbm,
    mom_hbm,
    new_mom,
    upd,
    grad,
    mom,
    core_out,
    core_in,
    x_out,
    x_in,
    rows,
    gram,
    gram_core,
    half,
    ry_in,
    ry_out,
    full,
    s_stack,
    q_stack,
    r_stack,
    t_stack,
    result,
    core_ss,
    core_rs,
    x_ss,
    x_rs,
    fwd_ss,
    fwd_rs,
    ret_ss,
    ret_rs,
    gc_ss,
    gc_rs,
    ry_ss,
    ry_rs,
    ay_ss,
    ay_rs,
    ac_ss,
    ac_rs,
    load_s,
    entered,
):
    dp = lax.axis_index("dp")
    ex = lax.axis_index("expert")
    h, c = dp // 2, dp % 2
    y, z, a = ex // 32, (ex // 2) % NZ, ex % 2

    other_core = (h * 2 + 1 - c, ex)
    x_partner = ((1 - h) * 2 + c, ex)

    def z_peer(i):
        return (h * 2 + a, y * 32 + i * 2 + c)

    def along_z(d):
        return (dp, y * 32 + ((z + d) % NZ) * 2 + a)

    def y_peer(k):
        return (dp, ((y + k) % NY) * 32 + z * 2 + a)

    def remote(src, dst, ss, rs, to):
        return pltpu.make_async_remote_copy(
            src_ref=src, dst_ref=dst, send_sem=ss, recv_sem=rs, device_id=to, device_id_type=MESH
        )

    straight = a == c

    loads = [
        pltpu.make_async_copy(grad_hbm, grad, load_s.at[0]),
        pltpu.make_async_copy(mom_hbm, mom, load_s.at[1]),
    ]
    for load in loads:
        load.start()

    pending = []

    def finish():
        for wait in pending:
            wait()

    def unless_here(s, then):
        pl.when(jnp.logical_not(jnp.logical_and(straight, z == s)))(then)

    barrier = pltpu.get_barrier_semaphore()

    def greet(to):
        pl.semaphore_signal(barrier, inc=1, device_id=to, device_id_type=MESH)

    greet(other_core)
    greet(x_partner)
    for k in range(1, NY):
        greet(y_peer(k))
    for d in (1, NZ - 1):
        greet(along_z(d))

    @pl.when(jnp.logical_not(straight))
    def _():
        for d in (0, 1, NZ - 1):
            greet(z_peer((z + d) % NZ))

    pl.semaphore_wait(barrier, 10 - 3 * straight.astype(jnp.int32))

    def hand_on(step):
        d = 2**step
        for away in (d, NZ - d):
            pl.semaphore_signal(entered.at[step], inc=1, device_id=along_z(away), device_id_type=MESH)
        pl.semaphore_wait(entered.at[step], 2)

    for load in loads:
        load.wait()

    def core_copy(side, w):
        return remote(core_out.at[side, w], core_in.at[side, w], core_ss.at[side, w], core_rs.at[side, w], other_core)

    def x_copy(w):
        return remote(x_out.at[w], x_in.at[w], x_ss.at[w], x_rs.at[w], x_partner)

    def base(side, core):
        owner_h = 1 - h if side == 0 else h
        return (owner_h * 2 + core) * EXP

    for side in range(2):
        for w in range(WAVES):
            for j in range(PER):
                core_out[side, w, j] = grad[0, base(side, 1 - c) + WAVES * j + w].astype(f32)
            core_copy(side, w).start()
            pending.append(core_copy(side, w).wait_send)

    def x_send(w):
        core_copy(0, w).wait_recv()
        for j in range(PER):
            x_out[w, j] = grad[0, base(0, c) + WAVES * j + w].astype(f32) + core_in[0, w, j]
        x_copy(w).start()
        pending.append(x_copy(w).wait_send)

    hand_on(0)
    for w in range(XAHEAD):
        x_send(w)
    hand_on(1)
    hand_on(2)

    def fwd_copy(i, slot):
        return remote(new_mom.at[i], rows.at[slot], fwd_ss.at[i], fwd_rs.at[slot], z_peer(i))

    for w in range(WAVES):
        core_copy(1, w).wait_recv()
        for j in range(PER):
            i = WAVES * j + w
            new_mom[i] = momentum_keep * mom[i] + (grad[0, base(1, c) + i].astype(f32) + core_in[1, w, j])
        x_copy(w).wait_recv()
        if w + XAHEAD < WAVES:
            x_send(w + XAHEAD)
        for j in range(PER):
            i = WAVES * j + w
            new_mom[i] = new_mom[i] + x_in[w, j]
        if w >= 1:

            @pl.when(z % WAVES >= w)
            def _():
                for j in range(PER):
                    i = WAVES * j + w - 1
                    unless_here(i, fwd_copy(i, i).wait_send)

        for j in range(PER):
            i = WAVES * j + w
            @pl.when(jnp.logical_and(straight, z == i))
            def _():
                rows[i] = new_mom[i]

            unless_here(i, fwd_copy(i, z).start)

    def fwd_finish():
        for w in range(WAVES):

            def left():
                for j in range(PER):
                    i = WAVES * j + w
                    unless_here(i, fwd_copy(i, i).wait_send)

            if w + 1 < WAVES:
                pl.when(z % WAVES < w + 1)(left)
            else:
                left()

    pending.append(fwd_finish)

    for s in range(NZ):

        @pl.when(jnp.logical_not(jnp.logical_and(straight, z == s)))
        def _():
            fwd_copy(s, s).wait_recv()

    x0 = rows[...].reshape(NZ * ROWS, FF)
    x_hi, x_lo = split(x0)
    left = jnp.concatenate([x_hi, x_hi, x_lo], axis=0)
    right = jnp.concatenate([x_hi, x_lo, x_hi], axis=0)
    for b, (p, q) in enumerate(PAIRS):
        gram[b] = dot_rows(left[:, p * BLK : (p + 1) * BLK], right[:, q * BLK : (q + 1) * BLK])

    gc = remote(gram.at[pl.ds(3 * (1 - c), 3)], gram_core, gc_ss, gc_rs, other_core)
    gc.start()
    pending.append(gc.wait_send)
    gc.wait_recv()
    for k in range(3):
        half[pl.ds(k * BLK, BLK)] = gram[3 * c + k] + gram_core[k]

    up, down = y_peer(1), y_peer(NY - 1)
    p_up, p_far, p_down = (y + 1) % NY, (y + 2) % NY, (y + NY - 1) % NY

    def part(p, side):
        return pl.ds(pl.multiple_of(p * PIECE + side * HALF_PIECE, HALF_PIECE), HALF_PIECE)

    def ry_copy(k, src, to):
        return remote(src, ry_in.at[k], ry_ss.at[k], ry_rs.at[k], to)

    ry = [
        ry_copy(0, half.at[part(p_far, 0)], up),
        ry_copy(1, half.at[part(p_far, 1)], down),
        ry_copy(2, half.at[part(p_up, 1)], up),
        ry_copy(3, half.at[part(p_down, 0)], down),
        ry_copy(4, ry_out.at[0], up),
        ry_copy(5, ry_out.at[1], down),
    ]
    for k in range(4):
        ry[k].start()
    for k, p in ((0, p_up), (1, p_down)):
        ry[k].wait_recv()
        ry_out[k] = ry_in[k] + half[part(p, k)]
        ry[4 + k].start()
    for k in range(2, 6):
        ry[k].wait_recv()
    full[c, part(y, 0)] = half[part(y, 0)] + (ry_in[3] + ry_in[4])
    full[c, part(y, 1)] = half[part(y, 1)] + (ry_in[2] + ry_in[5])
    for copy in ry:
        pending.append(copy.wait_send)

    def ay_copy(k, p, side, to):
        place = full.at[c, part(p, side)]
        return remote(place, place, ay_ss.at[k], ay_rs.at[k], to)

    arrivals = ((p_down, 0), (p_up, 1), (p_down, 1), (p_up, 0), (p_far, 0), (p_far, 1))

    def ac_copy(k, core):
        place = full.at[core, part(*arrivals[k])]
        return remote(place, place, ac_ss.at[k], ac_rs.at[k], other_core)

    def own_copy(core):
        place = full.at[core, pl.ds(pl.multiple_of(y * PIECE, PIECE), PIECE)]
        return remote(place, place, ac_ss.at[6], ac_rs.at[6], other_core)

    ay = [
        ay_copy(0, y, 0, up),
        ay_copy(1, y, 1, down),
        ay_copy(2, y, 1, up),
        ay_copy(3, y, 0, down),
        ay_copy(4, p_down, 0, up),
        ay_copy(5, p_up, 1, down),
    ]
    for k in range(4):
        ay[k].start()
    own_copy(c).start()
    for k in range(6):
        ay_copy(k, *arrivals[k], up).wait_recv()
        if k < 2:
            ay[4 + k].start()
        ac_copy(k, c).start()
    for k in range(6):
        ac_copy(k, 1 - c).wait_recv()
        pending.append(ay[k].wait_send)
        pending.append(ac_copy(k, c).wait_send)
    own_copy(1 - c).wait_recv()
    pending.append(own_copy(c).wait_send)

    def block(b):
        return full[b // 3, (b % 3) * BLK : (b % 3 + 1) * BLK, :]

    eye = lax.broadcasted_iota(jnp.int32, (BLK, BLK), 0) == lax.broadcasted_iota(jnp.int32, (BLK, BLK), 1)
    on_diagonal = jnp.where(eye, block(0) + block(3) + block(5), 0.0)
    square_sum = jnp.sum(jnp.sum(on_diagonal, axis=1, keepdims=True), axis=0, keepdims=True)
    factor = 1.0 / (jnp.sqrt(square_sum) + norm_epsilon)
    scale = factor * factor

    def put(stack, p, q, value):
        vh, vl = split(value)
        columns = slice(q * BLK, (q + 1) * BLK)
        for k, v in enumerate((vh, vl, vh)):
            stack[k * FF + p * BLK : k * FF + (p + 1) * BLK, columns] = v

    def put_both(stack, p, q, value):
        put(stack, p, q, value)
        if p != q:
            put(stack, q, p, value.T)

    def panels(stack):
        out = []
        for p in range(3):
            vh = stack[p * BLK : (p + 1) * BLK, :]
            vl = stack[FF + p * BLK : FF + (p + 1) * BLK, :]
            out.append(jnp.concatenate([vh, vh, vl], axis=1))
        return out

    def times(value, stack):
        vh, vl = split(value)
        return dot(jnp.concatenate([vh, vh, vl], axis=1), stack[...])

    for b, (p, q) in enumerate(PAIRS):
        put_both(s_stack, p, q, block(b) * scale)
    s_panels = panels(s_stack)
    for b, (p, q) in enumerate(PAIRS):
        square = dot(s_panels[p], s_stack[:, q * BLK : (q + 1) * BLK])
        value = (second_coeff * scale) * block(b) + third_coeff * square
        if p == q:
            value = value + jnp.where(eye, first_coeff, 0.0)
        put_both(q_stack, p, q, value)

    for b, (p, q) in enumerate(PAIRS):
        put_both(r_stack, p, q, dot(s_panels[p], q_stack[:, q * BLK : (q + 1) * BLK]))
    r_panels = panels(r_stack)
    for b, (p, q) in enumerate(PAIRS):
        put_both(t_stack, p, q, dot(r_panels[p], q_stack[:, q * BLK : (q + 1) * BLK]))
    x1 = times(x0, q_stack) * factor
    t1 = times(x1, t_stack)
    t2 = times(t1, t_stack)
    final = D**0.5 * (first_coeff * x1 + second_coeff * t1 + third_coeff * t2)
    result[...] = final.reshape(NZ, ROWS, FF)

    def ret_copy(s, slot):
        return remote(result.at[s], upd.at[slot], ret_ss.at[s], ret_rs.at[slot], z_peer(s))

    @pl.when(straight)
    def _():
        upd[z] = result[z]

    pl.when(jnp.logical_not(straight))(ret_copy(z, z).start)
    for k in [8, 7, 9, 6, 10, 5, 11, 4, 12, 3, 13, 2, 14, 1, 15]:
        ret_copy((z + k) % NZ, z).start()

    finish()
    for s in range(NZ):
        unless_here(s, ret_copy(s, s).wait_send)
        unless_here(s, ret_copy(s, s).wait_recv)


def shards(gradient, momentum):
    vmem = pl.BlockSpec(memory_space=pltpu.VMEM)
    dma = pltpu.SemaphoreType.DMA
    shape = jax.ShapeDtypeStruct(momentum.shape, f32)
    return pl.pallas_call(
        kernel,
        out_shape=(shape, shape),
        in_specs=[pl.BlockSpec(memory_space=pl.ANY)] * 2,
        out_specs=(vmem, vmem),
        scratch_shapes=[
            pltpu.VMEM(gradient.shape, bf16),
            pltpu.VMEM(momentum.shape, f32),
            pltpu.VMEM((2, WAVES, PER, ROWS, FF), f32),
            pltpu.VMEM((2, WAVES, PER, ROWS, FF), f32),
            pltpu.VMEM((WAVES, PER, ROWS, FF), f32),
            pltpu.VMEM((WAVES, PER, ROWS, FF), f32),
            pltpu.VMEM((NZ, ROWS, FF), f32),
            pltpu.VMEM((6, BLK, BLK), f32),
            pltpu.VMEM((3, BLK, BLK), f32),
            pltpu.VMEM((HALF, BLK), f32),
            pltpu.VMEM((6, HALF_PIECE, BLK), f32),
            pltpu.VMEM((2, HALF_PIECE, BLK), f32),
            pltpu.VMEM((2, HALF, BLK), f32),
            pltpu.VMEM((3 * FF, FF), bf16),
            pltpu.VMEM((3 * FF, FF), bf16),
            pltpu.VMEM((3 * FF, FF), bf16),
            pltpu.VMEM((3 * FF, FF), bf16),
            pltpu.VMEM((NZ, ROWS, FF), f32),
            dma((2, WAVES)),
            dma((2, WAVES)),
            dma((WAVES,)),
            dma((WAVES,)),
            dma((NZ,)),
            dma((NZ,)),
            dma((NZ,)),
            dma((NZ,)),
            dma,
            dma,
            dma((6,)),
            dma((6,)),
            dma((6,)),
            dma((6,)),
            dma((7,)),
            dma((7,)),
            dma((2,)),
            pltpu.SemaphoreType.REGULAR((3,)),
        ],
        compiler_params=pltpu.CompilerParams(
            collective_id=0, has_side_effects=True, vmem_limit_bytes=60 * 2**20
        ),
        name="muon",
    )(gradient, momentum)


def solution(mesh):
    placed = (P("dp", None, "expert", None), P("dp", "expert", None))
    return jax.shard_map(
        shards,
        mesh=mesh,
        in_specs=placed,
        out_specs=(P("dp", "expert", None), P("dp", "expert", None)),
        check_vma=False,
    )
```

time: 140 us -> 127 us (0.907)
  the two profiles are of different devices: /device:TPU:448 before, /device:TPU:32 now
where the time goes in v2:
time: 127 us
  Pallas kernels  124 us (98%)
  local copies, waits for them, and re-layouts  3.03 us (2%)
    pallas_call x1, Pallas kernels, shards(): pl.pallas_call(kernel, out_shape=(shape, shape), in_specs=[pl.BlockSpec(m...  124 us
    unnamed x4, local copies, waits for them, and re-layouts  3.03 us

profile of v2, /device:TPU:32, one launch (start us, length us, event | category | flops | bytes accessed | tf_op | source)
XLA Modules:
  0.0 127.3 jit_solution(3104350443600883579)
XLA Ops:
  0.6 123.6 %muon.1 = (f32[16,16,768]{2,1,0:T(8,128)}, f32[16,16,768]{2,1,0:T(8,128)}) custom-call(bf16[1,64,16,768]{3,2,1,0:T(8,128)(2,1)} %grad_hbm.1, f32[16,16,768]{2,1,0:T(8,128)} %mom_hbm.1), custom_call_target="tpu_custom_call" | custom-call | tf_op jit(solution)/shard_map/muon/pallas_call | solution.py:396
  124.3 0.0 copy-start
  124.3 2.1 %copy.6 = f32[16,16,768]{2,1,0:T(8,128)} copy(f32[16,16,768]{2,1,0:T(8,128)} %get-tuple-element.4) | data formatting | bytes 1572864
  126.4 0.0 copy-done
  126.4 0.9 copy.7
Async XLA Ops:
  124.3 2.2 %copy-start = (f32[16,16,768]{2,1,0:T(8,128)S(1)}, f32[16,16,768]{2,1,0:T(8,128)}, u32[]{:S(2)}) copy-start(f32[16,16,768]{2,1,0:T(8,128)} %get-tuple-element.5) | copy-start | bytes 2359300

commit v3 on v2

--- a/solution.py
+++ b/solution.py
@@ -21,17 +21,23 @@
 ROWS = 16
 WAVES = 4
 PER = EXP // WAVES
+ORDER = (0, 2, 1, 3)
 BLK = 256
 PAIRS = ((0, 0), (0, 1), (0, 2), (1, 1), (1, 2), (2, 2))
 DIAGONAL = (0, 3, 5)
-HALF = 3 * BLK
-PIECE = HALF // NY
+PIECE = BLK // NY
 HALF_PIECE = PIECE // 2
 
+PARTS = 2
+GC = 1
 XAHEAD = 2
 MESH = pl.DeviceIdType.MESH
 f32 = jnp.float32
 bf16 = jnp.bfloat16
+
+
+def wave_of(i):
+    return (i % 2) * 2 + (i // 2) % 2
 
 
 def split(value):
@@ -88,6 +94,7 @@
     ac_rs,
     load_s,
     entered,
+    go,
 ):
     dp = lax.axis_index("dp")
     ex = lax.axis_index("expert")
@@ -113,12 +120,18 @@
 
     straight = a == c
 
-    loads = [
-        pltpu.make_async_copy(grad_hbm, grad, load_s.at[0]),
-        pltpu.make_async_copy(mom_hbm, mom, load_s.at[1]),
-    ]
-    for load in loads:
-        load.start()
+    def base(side, core):
+        owner_h = 1 - h if side == 0 else h
+        return (owner_h * 2 + core) * EXP
+
+    def grad_load(k):
+        quarter = pl.ds(pl.multiple_of(base(k // 2, 1 - c if k % 2 == 0 else c), EXP), EXP)
+        return pltpu.make_async_copy(grad_hbm.at[0, quarter], grad.at[0, quarter], load_s.at[k])
+
+    mom_load = pltpu.make_async_copy(mom_hbm, mom, load_s.at[4])
+    for k in range(4):
+        grad_load(k).start()
+    mom_load.start()
 
     pending = []
 
@@ -152,10 +165,9 @@
         d = 2**step
         for away in (d, NZ - d):
             pl.semaphore_signal(entered.at[step], inc=1, device_id=along_z(away), device_id_type=MESH)
+
+    def heard(step):
         pl.semaphore_wait(entered.at[step], 2)
-
-    for load in loads:
-        load.wait()
 
     def core_copy(side, w):
         return remote(core_out.at[side, w], core_in.at[side, w], core_ss.at[side, w], core_rs.at[side, w], other_core)
@@ -163,80 +175,111 @@
     def x_copy(w):
         return remote(x_out.at[w], x_in.at[w], x_ss.at[w], x_rs.at[w], x_partner)
 
-    def base(side, core):
-        owner_h = 1 - h if side == 0 else h
-        return (owner_h * 2 + core) * EXP
-
     for side in range(2):
+        grad_load(2 * side).wait()
         for w in range(WAVES):
             for j in range(PER):
-                core_out[side, w, j] = grad[0, base(side, 1 - c) + WAVES * j + w].astype(f32)
+                core_out[side, w, j] = grad[0, base(side, 1 - c) + WAVES * j + ORDER[w]].astype(f32)
             core_copy(side, w).start()
             pending.append(core_copy(side, w).wait_send)
 
     def x_send(w):
         core_copy(0, w).wait_recv()
         for j in range(PER):
-            x_out[w, j] = grad[0, base(0, c) + WAVES * j + w].astype(f32) + core_in[0, w, j]
+            x_out[w, j] = grad[0, base(0, c) + WAVES * j + ORDER[w]].astype(f32) + core_in[0, w, j]
         x_copy(w).start()
         pending.append(x_copy(w).wait_send)
 
     hand_on(0)
+    heard(0)
+    hand_on(1)
+    grad_load(1).wait()
     for w in range(XAHEAD):
         x_send(w)
-    hand_on(1)
+    heard(1)
     hand_on(2)
+    grad_load(3).wait()
+    mom_load.wait()
 
     def fwd_copy(i, slot):
         return remote(new_mom.at[i], rows.at[slot], fwd_ss.at[i], fwd_rs.at[slot], z_peer(i))
+
+    def rows_wait():
+        for s in range(NZ):
+            unless_here(s, fwd_copy(s, s).wait_recv)
+
+    def tell(i, wave):
+        pl.semaphore_signal(go.at[wave], inc=1, device_id=z_peer(i), device_id_type=MESH)
 
     for w in range(WAVES):
         core_copy(1, w).wait_recv()
         for j in range(PER):
-            i = WAVES * j + w
+            i = WAVES * j + ORDER[w]
             new_mom[i] = momentum_keep * mom[i] + (grad[0, base(1, c) + i].astype(f32) + core_in[1, w, j])
         x_copy(w).wait_recv()
         if w + XAHEAD < WAVES:
             x_send(w + XAHEAD)
         for j in range(PER):
-            i = WAVES * j + w
+            i = WAVES * j + ORDER[w]
             new_mom[i] = new_mom[i] + x_in[w, j]
-        if w >= 1:
-
-            @pl.when(z % WAVES >= w)
+        if w == 1:
+
+            @pl.when(wave_of(z) >= GC)
             def _():
                 for j in range(PER):
-                    i = WAVES * j + w - 1
+                    i = WAVES * j + ORDER[0]
                     unless_here(i, fwd_copy(i, i).wait_send)
 
+        if w >= 2:
+            done = w - 2
+
+            @pl.when(wave_of(z) == done)
+            def _():
+                rows_wait()
+                for i in range(NZ):
+                    if wave_of(i) > done:
+                        unless_here(i, functools.partial(tell, i, done))
+
+            @pl.when(wave_of(z) > done)
+            def _():
+                pl.semaphore_wait(go.at[done], PER)
+
         for j in range(PER):
-            i = WAVES * j + w
+            i = WAVES * j + ORDER[w]
+
             @pl.when(jnp.logical_and(straight, z == i))
             def _():
                 rows[i] = new_mom[i]
 
-            unless_here(i, fwd_copy(i, z).start)
+        if w > 0:
+            for j in range(PER):
+                i = WAVES * j + ORDER[w]
+                unless_here(i, fwd_copy(i, z).start)
+        else:
+            for j in range(PER):
+                i = WAVES * j + ORDER[w]
+                pl.when((i - z + 4 + NZ) % NZ <= 8)(functools.partial(unless_here, i, fwd_copy(i, z).start))
+            heard(2)
+            for j in range(PER):
+                i = WAVES * j + ORDER[w]
+                pl.when((i - z + 4 + NZ) % NZ > 8)(fwd_copy(i, z).start)
 
     def fwd_finish():
         for w in range(WAVES):
 
             def left():
                 for j in range(PER):
-                    i = WAVES * j + w
+                    i = WAVES * j + ORDER[w]
                     unless_here(i, fwd_copy(i, i).wait_send)
 
-            if w + 1 < WAVES:
-                pl.when(z % WAVES < w + 1)(left)
+            if w == 0:
+                pl.when(wave_of(z) < GC)(left)
             else:
                 left()
 
     pending.append(fwd_finish)
 
-    for s in range(NZ):
-
-        @pl.when(jnp.logical_not(jnp.logical_and(straight, z == s)))
-        def _():
-            fwd_copy(s, s).wait_recv()
+    pl.when(wave_of(z) >= 2)(rows_wait)
 
     x0 = rows[...].reshape(NZ * ROWS, FF)
     x_hi, x_lo = split(x0)
@@ -245,82 +288,97 @@
     for b, (p, q) in enumerate(PAIRS):
         gram[b] = dot_rows(left[:, p * BLK : (p + 1) * BLK], right[:, q * BLK : (q + 1) * BLK])
 
-    gc = remote(gram.at[pl.ds(3 * (1 - c), 3)], gram_core, gc_ss, gc_rs, other_core)
-    gc.start()
-    pending.append(gc.wait_send)
-    gc.wait_recv()
-    for k in range(3):
-        half[pl.ds(k * BLK, BLK)] = gram[3 * c + k] + gram_core[k]
-
     up, down = y_peer(1), y_peer(NY - 1)
     p_up, p_far, p_down = (y + 1) % NY, (y + 2) % NY, (y + NY - 1) % NY
 
     def part(p, side):
         return pl.ds(pl.multiple_of(p * PIECE + side * HALF_PIECE, HALF_PIECE), HALF_PIECE)
 
-    def ry_copy(k, src, to):
-        return remote(src, ry_in.at[k], ry_ss.at[k], ry_rs.at[k], to)
+    def gc_copy(k):
+        return remote(gram.at[3 * (1 - c) + k], gram_core.at[k], gc_ss.at[k], gc_rs.at[k], other_core)
+
+    def ry_copy(k, n, src, to):
+        return remote(src, ry_in.at[k, n], ry_ss.at[k, n], ry_rs.at[k, n], to)
 
     ry = [
-        ry_copy(0, half.at[part(p_far, 0)], up),
-        ry_copy(1, half.at[part(p_far, 1)], down),
-        ry_copy(2, half.at[part(p_up, 1)], up),
-        ry_copy(3, half.at[part(p_down, 0)], down),
-        ry_copy(4, ry_out.at[0], up),
-        ry_copy(5, ry_out.at[1], down),
+        [
+            ry_copy(k, 0, half.at[k, part(p_far, 0)], up),
+            ry_copy(k, 1, half.at[k, part(p_far, 1)], down),
+            ry_copy(k, 2, half.at[k, part(p_up, 1)], up),
+            ry_copy(k, 3, half.at[k, part(p_down, 0)], down),
+            ry_copy(k, 4, ry_out.at[k, 0], up),
+            ry_copy(k, 5, ry_out.at[k, 1], down),
+        ]
+        for k in range(3)
     ]
-    for k in range(4):
-        ry[k].start()
-    for k, p in ((0, p_up), (1, p_down)):
-        ry[k].wait_recv()
-        ry_out[k] = ry_in[k] + half[part(p, k)]
-        ry[4 + k].start()
-    for k in range(2, 6):
-        ry[k].wait_recv()
-    full[c, part(y, 0)] = half[part(y, 0)] + (ry_in[3] + ry_in[4])
-    full[c, part(y, 1)] = half[part(y, 1)] + (ry_in[2] + ry_in[5])
-    for copy in ry:
-        pending.append(copy.wait_send)
-
-    def ay_copy(k, p, side, to):
-        place = full.at[c, part(p, side)]
-        return remote(place, place, ay_ss.at[k], ay_rs.at[k], to)
+
+    def ay_copy(k, n, p, side, to):
+        place = full.at[c, k, part(p, side)]
+        return remote(place, place, ay_ss.at[k, n], ay_rs.at[k, n], to)
 
     arrivals = ((p_down, 0), (p_up, 1), (p_down, 1), (p_up, 0), (p_far, 0), (p_far, 1))
 
-    def ac_copy(k, core):
-        place = full.at[core, part(*arrivals[k])]
-        return remote(place, place, ac_ss.at[k], ac_rs.at[k], other_core)
-
-    def own_copy(core):
-        place = full.at[core, pl.ds(pl.multiple_of(y * PIECE, PIECE), PIECE)]
-        return remote(place, place, ac_ss.at[6], ac_rs.at[6], other_core)
+    def ac_copy(k, n, core):
+        place = full.at[core, k, part(*arrivals[n])]
+        return remote(place, place, ac_ss.at[k, n], ac_rs.at[k, n], other_core)
+
+    def own_copy(k, core):
+        place = full.at[core, k, pl.ds(pl.multiple_of(y * PIECE, PIECE), PIECE)]
+        return remote(place, place, ac_ss.at[k, 6], ac_rs.at[k, 6], other_core)
 
     ay = [
-        ay_copy(0, y, 0, up),
-        ay_copy(1, y, 1, down),
-        ay_copy(2, y, 1, up),
-        ay_copy(3, y, 0, down),
-        ay_copy(4, p_down, 0, up),
-        ay_copy(5, p_up, 1, down),
+        [
+            ay_copy(k, 0, y, 0, up),
+            ay_copy(k, 1, y, 1, down),
+            ay_copy(k, 2, y, 1, up),
+            ay_copy(k, 3, y, 0, down),
+            ay_copy(k, 4, p_down, 0, up),
+            ay_copy(k, 5, p_up, 1, down),
+        ]
+        for k in range(3)
     ]
-    for k in range(4):
-        ay[k].start()
-    own_copy(c).start()
-    for k in range(6):
-        ay_copy(k, *arrivals[k], up).wait_recv()
-        if k < 2:
-            ay[4 + k].start()
-        ac_copy(k, c).start()
-    for k in range(6):
-        ac_copy(k, 1 - c).wait_recv()
-        pending.append(ay[k].wait_send)
-        pending.append(ac_copy(k, c).wait_send)
-    own_copy(1 - c).wait_recv()
-    pending.append(own_copy(c).wait_send)
+
+    for k in range(3):
+        gc_copy(k).start()
+    for k in range(3):
+        gc_copy(k).wait_recv()
+        half[k] = gram[3 * c + k] + gram_core[k]
+        for n in range(4):
+            ry[k][n].start()
+    for k in range(3):
+        for n, p in ((0, p_up), (1, p_down)):
+            ry[k][n].wait_recv()
+            ry_out[k, n] = ry_in[k, n] + half[k, part(p, n)]
+            ry[k][4 + n].start()
+    for k in range(3):
+        for n in range(2, 6):
+            ry[k][n].wait_recv()
+        full[c, k, part(y, 0)] = half[k, part(y, 0)] + (ry_in[k, 3] + ry_in[k, 4])
+        full[c, k, part(y, 1)] = half[k, part(y, 1)] + (ry_in[k, 2] + ry_in[k, 5])
+        for n in range(4):
+            ay[k][n].start()
+        own_copy(k, c).start()
+    for k in range(3):
+        for n in range(2):
+            ay_copy(k, n, *arrivals[n], up).wait_recv()
+            ay[k][4 + n].start()
+            ac_copy(k, n, c).start()
+    for k in range(3):
+        for n in range(2, 6):
+            ay_copy(k, n, *arrivals[n], up).wait_recv()
+            ac_copy(k, n, c).start()
+    for k in range(3):
+        own_copy(k, 1 - c).wait_recv()
+        pending.append(own_copy(k, c).wait_send)
+        pending.append(gc_copy(k).wait_send)
+        for n in range(6):
+            ac_copy(k, n, 1 - c).wait_recv()
+            pending.append(ry[k][n].wait_send)
+            pending.append(ay[k][n].wait_send)
+            pending.append(ac_copy(k, n, c).wait_send)
 
     def block(b):
-        return full[b // 3, (b % 3) * BLK : (b % 3 + 1) * BLK, :]
+        return full[b // 3, b % 3]
 
     eye = lax.broadcasted_iota(jnp.int32, (BLK, BLK), 0) == lax.broadcasted_iota(jnp.int32, (BLK, BLK), 1)
     on_diagonal = jnp.where(eye, block(0) + block(3) + block(5), 0.0)
@@ -366,22 +424,24 @@
     r_panels = panels(r_stack)
     for b, (p, q) in enumerate(PAIRS):
         put_both(t_stack, p, q, dot(r_panels[p], q_stack[:, q * BLK : (q + 1) * BLK]))
-    x1 = times(x0, q_stack) * factor
-    t1 = times(x1, t_stack)
-    t2 = times(t1, t_stack)
-    final = D**0.5 * (first_coeff * x1 + second_coeff * t1 + third_coeff * t2)
-    result[...] = final.reshape(NZ, ROWS, FF)
 
     def ret_copy(s, slot):
         return remote(result.at[s], upd.at[slot], ret_ss.at[s], ret_rs.at[slot], z_peer(s))
 
-    @pl.when(straight)
-    def _():
-        upd[z] = result[z]
-
-    pl.when(jnp.logical_not(straight))(ret_copy(z, z).start)
-    for k in [8, 7, 9, 6, 10, 5, 11, 4, 12, 3, 13, 2, 14, 1, 15]:
-        ret_copy((z + k) % NZ, z).start()
+    for first in range(0, NZ, NZ // PARTS):
+        slots = range(first, first + NZ // PARTS)
+        x1 = times(x0[first * ROWS : (first + NZ // PARTS) * ROWS], q_stack) * factor
+        t1 = times(x1, t_stack)
+        t2 = times(t1, t_stack)
+        final = D**0.5 * (first_coeff * x1 + second_coeff * t1 + third_coeff * t2)
+        result[first : first + NZ // PARTS] = final.reshape(NZ // PARTS, ROWS, FF)
+        for s in slots:
+
+            @pl.when(jnp.logical_and(straight, z == s))
+            def _():
+                upd[s] = result[s]
+
+            unless_here(s, ret_copy(s, z).start)
 
     finish()
     for s in range(NZ):
@@ -408,10 +468,10 @@
             pltpu.VMEM((NZ, ROWS, FF), f32),
             pltpu.VMEM((6, BLK, BLK), f32),
             pltpu.VMEM((3, BLK, BLK), f32),
-            pltpu.VMEM((HALF, BLK), f32),
-            pltpu.VMEM((6, HALF_PIECE, BLK), f32),
-            pltpu.VMEM((2, HALF_PIECE, BLK), f32),
-            pltpu.VMEM((2, HALF, BLK), f32),
+            pltpu.VMEM((3, BLK, BLK), f32),
+            pltpu.VMEM((3, 6, HALF_PIECE, BLK), f32),
+            pltpu.VMEM((3, 2, HALF_PIECE, BLK), f32),
+            pltpu.VMEM((2, 3, BLK, BLK), f32),
             pltpu.VMEM((3 * FF, FF), bf16),
             pltpu.VMEM((3 * FF, FF), bf16),
             pltpu.VMEM((3 * FF, FF), bf16),
@@ -425,19 +485,20 @@
             dma((NZ,)),
             dma((NZ,)),
             dma((NZ,)),
-            dma,
-            dma,
-            dma((6,)),
-            dma((6,)),
-            dma((6,)),
-            dma((6,)),
-            dma((7,)),
-            dma((7,)),
-            dma((2,)),
+            dma((3,)),
+            dma((3,)),
+            dma((3, 6)),
+            dma((3, 6)),
+            dma((3, 6)),
+            dma((3, 6)),
+            dma((3, 7)),
+            dma((3, 7)),
+            dma((5,)),
             pltpu.SemaphoreType.REGULAR((3,)),
+            pltpu.SemaphoreType.REGULAR((WAVES - 2,)),
         ],
         compiler_params=pltpu.CompilerParams(
-            collective_id=0, has_side_effects=True, vmem_limit_bytes=60 * 2**20
+            collective_id=0, has_side_effects=True, vmem_limit_bytes=52 * 2**20
         ),
         name="muon",
     )(gradient, momentum)

time: 127 us -> 119 us (0.937)
  the two profiles are of different devices: /device:TPU:32 before, /device:TPU:454 now
where the time goes in v3:
time: 119 us
  Pallas kernels  117 us (98%)
  local copies, waits for them, and re-layouts  1.76 us (1%)
    pallas_call x1, Pallas kernels, shards(): pl.pallas_call(kernel, out_shape=(shape, shape), in_specs=[pl.BlockSpec(m...  117 us

profile of v3, /device:TPU:454, one launch (start us, length us, event | category | flops | bytes accessed | tf_op | source)
XLA Modules:
  0.0 119.1 jit_solution(759243294559650907)
XLA Ops:
  0.6 116.7 %muon.1 = (f32[16,16,768]{2,1,0:T(8,128)S(1)}, f32[16,16,768]{2,1,0:T(8,128)S(1)}) custom-call(bf16[1,64,16,768]{3,2,1,0:T(8,128)(2,1)} %grad_hbm.1, f32[16,16,768]{2,1,0:T(8,128)} %mom_hbm.1), custom_call_target="tpu_custom_call" | custom-call | tf_op jit(solution)/shard_map/muon/pallas_call | solution.py:456
  117.4 0.9 copy.6
  118.2 0.9 copy.7

commit v4 on v3

--- a/solution.py
+++ b/solution.py
@@ -30,7 +30,7 @@
 
 PARTS = 2
 GC = 1
-XAHEAD = 2
+XAHEAD = 3
 MESH = pl.DeviceIdType.MESH
 f32 = jnp.float32
 bf16 = jnp.bfloat16
@@ -285,9 +285,6 @@
     x_hi, x_lo = split(x0)
     left = jnp.concatenate([x_hi, x_hi, x_lo], axis=0)
     right = jnp.concatenate([x_hi, x_lo, x_hi], axis=0)
-    for b, (p, q) in enumerate(PAIRS):
-        gram[b] = dot_rows(left[:, p * BLK : (p + 1) * BLK], right[:, q * BLK : (q + 1) * BLK])
-
     up, down = y_peer(1), y_peer(NY - 1)
     p_up, p_far, p_down = (y + 1) % NY, (y + 2) % NY, (y + NY - 1) % NY
 
@@ -339,6 +336,9 @@
     ]
 
     for k in range(3):
+        for b in (k, 3 + k):
+            p, q = PAIRS[b]
+            gram[b] = dot_rows(left[:, p * BLK : (p + 1) * BLK], right[:, q * BLK : (q + 1) * BLK])
         gc_copy(k).start()
     for k in range(3):
         gc_copy(k).wait_recv()

time: 119 us -> 119 us (level)
  the two profiles are of different devices: /device:TPU:454 before, /device:TPU:453 now
where the time goes in v4:
time: 119 us
  Pallas kernels  116 us (97%)
  local copies, waits for them, and re-layouts  1.76 us (1%)
    pallas_call x1, Pallas kernels, shards(): pl.pallas_call(kernel, out_shape=(shape, shape), in_specs=[pl.BlockSpec(m...  116 us

profile of v4, /device:TPU:453, one launch (start us, length us, event | category | flops | bytes accessed | tf_op | source)
XLA Modules:
  0.0 118.8 jit_solution(12808856827053572026)
XLA Ops:
  0.6 116.4 %muon.1 = (f32[16,16,768]{2,1,0:T(8,128)S(1)}, f32[16,16,768]{2,1,0:T(8,128)S(1)}) custom-call(bf16[1,64,16,768]{3,2,1,0:T(8,128)(2,1)} %grad_hbm.1, f32[16,16,768]{2,1,0:T(8,128)} %mom_hbm.1), custom_call_target="tpu_custom_call" | custom-call | tf_op jit(solution)/shard_map/muon/pallas_call | solution.py:456
  117.0 0.9 copy.6
  117.9 0.9 copy.7
